TPU v7x, 512 devices: a whole 4x4x16 slice. The times are simulated.
512 devices in a mesh: ctx: 64 (over y, z), tp: 8 (over x, core).
Axes of the slice: x: 4, y: 4, z: 16, core: 2. Of those that a mesh axis runs over, the one named last changes fastest.
Arguments:
- lin_query: bfloat16 [8192, 4096], P('ctx', 'tp'), may hold values from -6 to 6
- lin_key: bfloat16 [8192, 4096], P('ctx', 'tp'), may hold values from -6 to 6
- lin_value: bfloat16 [8192, 4096], P('ctx', 'tp'), may hold values from -6 to 6
- lin_cotangent: bfloat16 [8192, 4096], P('ctx', 'tp'), may hold values from -6 to 6
- soft_query: bfloat16 [8192, 4096], P('ctx', 'tp'), may hold values from -200 to 200
- soft_key: bfloat16 [8192, 1024], P('ctx', 'tp'), may hold values from -200 to 200
- soft_value: bfloat16 [8192, 1024], P('ctx', 'tp'), may hold values from -6 to 6
- doc_start: int32 [8192], P('ctx'), may hold values from 0 to 8191, as said below
Outputs:
- lin_out: bfloat16 [8192, 4096], P('ctx', 'tp')
- grad_query: bfloat16 [8192, 4096], P('ctx', 'tp')
- grad_key: bfloat16 [8192, 4096], P('ctx', 'tp')
- grad_value: bfloat16 [8192, 4096], P('ctx', 'tp')
- soft_out: bfloat16 [8192, 4096], P('ctx', 'tp')
Inputs may be any that keep to these rules, and one draw needn't show every extreme that they name: doc_start[i] <= i, doc_start never falls along the sequence, doc_start[0] = 0, doc_start[i] equals i or doc_start[i - 1], and a document of one position starts at position 8191.
All inputs are finite; a program needn't handle non-finite values.
Results may differ from a plain program's by a relative error of at most 0.011.
Values may be sent and summed in bfloat16 or wider, within the bound.
No kernel may reach another device: no remote copies, remote signals or barrier semaphores. Data moves between devices by JAX's collectives and lax.ppermute only.
A program may use at most 128 MiB of HBM per device.

v0:
```python
import math
import jax
import jax.numpy as jnp
from jax import lax
from jax.sharding import PartitionSpec as P

HD = 128
LH = 32
SH = 32
KVH = 8
epsilon = 1e-06
highest = lax.Precision.HIGHEST
floor_score = -1e30


def carried_in(value, axis, combine, identity, reverse):
    length, position = (lax.axis_size(axis), lax.axis_index(axis))
    everything = lax.all_gather(value.astype(jnp.bfloat16), axis)
    start = jnp.broadcast_to(jnp.asarray(identity, value.dtype), value.shape)

    def hop(k, before):
        at = length - 1 - k if reverse else k
        reached = at > position if reverse else at < position
        new = combine(before, everything[at].astype(value.dtype))
        return jnp.where(reached, new, before)

    return lax.fori_loop(0, length, hop, start)


def on_device(
    lin_query, lin_key, lin_value, lin_cotangent, soft_query, soft_key, soft_value, doc_start
):
    length = lin_query.shape[0]
    heads_here = lin_query.shape[1] // HD
    queries = lin_query.reshape(length, heads_here, HD)
    keys = lin_key.reshape(length, heads_here, HD)
    values = lin_value.reshape(length, heads_here, HD)
    lower = jnp.tril(jnp.ones((length, length), dtype=bool))
    raw_scores = jnp.einsum("thd,shd->hts", queries, keys, preferred_element_type=jnp.float32)
    weights = jnp.where(lower[None], raw_scores, 0.0).astype(jnp.bfloat16)
    own_state = jnp.einsum("thd,the->hde", keys, values, preferred_element_type=jnp.float32)
    earlier = carried_in(own_state, "ctx", jnp.add, jnp.zeros_like(own_state), False)
    mixed = jnp.einsum("hts,shd->thd", weights, values, preferred_element_type=jnp.float32)
    mixed = mixed + jnp.einsum(
        "thd,hde->the", queries.astype(jnp.float32), earlier, precision=highest
    )
    mixed = mixed.reshape(length, heads_here * HD)
    squares = lax.psum(jnp.sum(mixed * mixed, axis=1), "tp")
    scale = lax.rsqrt(squares / (LH * HD) + epsilon)
    normed = mixed * scale[:, None]
    lin_out = normed.astype(jnp.bfloat16)
    grad = lin_cotangent.astype(jnp.float32)
    inner = lax.psum(jnp.sum(grad * normed, axis=1), "tp")
    grad_mix = scale[:, None] * (grad - normed * (inner / (LH * HD))[:, None])
    grad_mix = grad_mix.astype(jnp.bfloat16).reshape(length, heads_here, HD)
    own_adjoint = jnp.einsum("thd,the->hde", queries, grad_mix, preferred_element_type=jnp.float32)
    later = carried_in(own_adjoint, "ctx", jnp.add, jnp.zeros_like(own_adjoint), True)
    raw_grad = jnp.einsum("the,she->hts", grad_mix, values, preferred_element_type=jnp.float32)
    grad_scores = jnp.where(lower[None], raw_grad, 0.0).astype(jnp.bfloat16)
    grad_q = jnp.einsum("hts,shd->thd", grad_scores, keys, preferred_element_type=jnp.float32)
    grad_q = grad_q + jnp.einsum(
        "the,hde->thd", grad_mix.astype(jnp.float32), earlier, precision=highest
    )
    grad_k = jnp.einsum("hts,thd->shd", grad_scores, queries, preferred_element_type=jnp.float32)
    grad_k = grad_k + jnp.einsum(
        "she,hde->shd", values.astype(jnp.float32), later, precision=highest
    )
    grad_v = jnp.einsum("hts,thd->shd", weights, grad_mix, preferred_element_type=jnp.float32)
    grad_v = grad_v + jnp.einsum("shd,hde->she", keys.astype(jnp.float32), later, precision=highest)
    grad_query = grad_q.reshape(length, heads_here * HD).astype(jnp.bfloat16)
    grad_key = grad_k.reshape(length, heads_here * HD).astype(jnp.bfloat16)
    grad_value = grad_v.reshape(length, heads_here * HD).astype(jnp.bfloat16)
    group = SH // KVH
    kv_here = soft_key.shape[1] // HD
    factor = 1.0 / math.sqrt(HD)
    soft_q = soft_query.reshape(length, kv_here, group, HD)
    my_first = lax.axis_index("ctx") * length
    query_pos = my_first + jnp.arange(length, dtype=jnp.int32)

    def attend(carry, key_rows, value_rows, start):
        count = key_rows.shape[0]
        key_pos = start + jnp.arange(count, dtype=jnp.int32)
        allowed = (key_pos[None, :] <= query_pos[:, None]) & (
            key_pos[None, :] >= doc_start[:, None]
        )
        key_heads = key_rows.reshape(count, kv_here, HD)
        value_heads = value_rows.reshape(count, kv_here, HD)
        scores = (
            jnp.einsum("tkgd,nkd->kgtn", soft_q, key_heads, preferred_element_type=jnp.float32)
            * factor
        )
        scores = jnp.where(allowed, scores, floor_score)
        old_top, old_total, old_acc = carry
        new_top = jnp.maximum(old_top, jnp.max(scores, axis=-1))
        probs = jnp.where(allowed, jnp.exp(scores - new_top[..., None]), 0.0)
        shrink = jnp.exp(old_top - new_top)
        new_total = shrink * old_total + jnp.sum(probs, axis=-1)
        update = jnp.einsum(
            "kgtn,nkd->kgtd",
            probs.astype(jnp.bfloat16),
            value_heads,
            preferred_element_type=jnp.float32,
        )
        return (new_top, new_total, shrink[..., None] * old_acc + update)

    def visit(carry, key_rows, value_rows, start):
        return attend(carry, key_rows, value_rows, start)

    initial = (
        jnp.full((kv_here, group, length), floor_score, jnp.float32),
        jnp.zeros((kv_here, group, length), jnp.float32),
        jnp.zeros((kv_here, group, length, HD), jnp.float32),
    )
    key_rows = lax.all_gather(soft_key, "ctx", axis=0, tiled=True)
    value_rows = lax.all_gather(soft_value, "ctx", axis=0, tiled=True)
    count = key_rows.shape[0]
    block = math.gcd(count, 512)

    def inner_step(index, state):
        key_part = lax.dynamic_slice_in_dim(key_rows, index * block, block, 0)
        value_part = lax.dynamic_slice_in_dim(value_rows, index * block, block, 0)
        return visit(state, key_part, value_part, index * block)

    final = lax.fori_loop(0, count // block, inner_step, initial)
    top, total, accum = final
    result = accum / total[..., None]
    soft_out = (
        jnp.transpose(result, (2, 0, 1, 3))
        .reshape(length, kv_here * group * HD)
        .astype(jnp.bfloat16)
    )
    return (lin_out, grad_query, grad_key, grad_value, soft_out)


def solution(mesh):
    placed = (
        P("ctx", "tp"),
        P("ctx", "tp"),
        P("ctx", "tp"),
        P("ctx", "tp"),
        P("ctx", "tp"),
        P("ctx", "tp"),
        P("ctx", "tp"),
        P("ctx"),
    )
    return jax.shard_map(
        on_device,
        mesh=mesh,
        in_specs=placed,
        out_specs=(P("ctx", "tp"), P("ctx", "tp"), P("ctx", "tp"), P("ctx", "tp"), P("ctx", "tp")),
        check_vma=False,
    )
```

profile of v0, /device:TPU:2, one launch (start us, length us, event | category | flops | bytes accessed | tf_op | source)
XLA Modules:
  0.0 685.3 jit_solution(14521103591499810169)
XLA Ops:
  8.3 1.7 convolution_convert_fusion.1
  15.1 157.9 %all-gather.11.cloned.1.call-done = bf16[256,128,128]{2,1,0:T(8,128)(2,1)} async-done(((bf16[4,128,128]{2,1,0:T(8,128)(2,1)}), bf16[256,128,128]{2,1,0:T(8,128)(2,1)}) %all-gather.11.cloned.1.call-update) | async-done | bytes 8388624 | tf_op jit(solution)/shard_map/all_gather | solution.py:18
  173.0 67.9 %while.48 = (s32[]{:T(128)}, f32[4,128,128]{2,1,0:T(8,128)S(1)}, s32[]{:T(128)}, bf16[64,4,128,128]{3,2,1,0:T(8,128)(2,1)}, s32[]{:T(128)}, /*index=5*/s32[]{:T(128)}) while((s32[]{:T(128)}, f32[4,128,128]{2,1,0:T(8,128)S(1)}, s32[]{:T(128)}, bf16[64,4,128,128]{3,2,1,0:T(8,128)(2,1)}, s32[]{:T(128)}, /*index=5*/s32[]{:T(128)}) %tuple.131), condition=%wide.region_1.2_spmd.clone, body=%wide.region_0.1_spmd.clone.sunk | while | flops 262148 | bytes 655453 | solution.py:27
  241.5 10.0 %psum.14 = f32[128]{0:T(128)S(1)} all-reduce(f32[128]{0:T(128)S(1)} %get-tuple-element.497), channel_id=1, replica_groups=mesh['ctx'=64,'tp'=8] {'tp'}, use_global_device_ids=true, to_apply=%region_3.4 | all-reduce | flops 128 | bytes 1024 | tf_op jit(solution)/shard_map/psum | solution.py:48
  251.7 13.2 %psum.15 = f32[128]{0:T(128)S(1)} all-reduce(f32[128]{0:T(128)S(1)} %fusion.30), channel_id=1, replica_groups=mesh['ctx'=64,'tp'=8] {'tp'}, use_global_device_ids=true, to_apply=%region_5.6 | all-reduce | flops 128 | bytes 1024 | tf_op jit(solution)/shard_map/psum | solution.py:53
  266.8 45.0 %all-gather.7.cloned.1.call-done = bf16[8192,128]{1,0:T(8,128)(2,1)} async-done(((bf16[128,128]{1,0:T(8,128)(2,1)}), bf16[8192,128]{1,0:T(8,128)(2,1)}) %all-gather.7.cloned.1.call-update) | async-done | bytes 2097168 | tf_op jit(solution)/shard_map/all_gather | solution.py:114
  311.8 139.9 %all-gather.9.cloned.1.call-done = bf16[8192,128]{1,0:T(8,128)(2,1)} async-done(((bf16[128,128]{1,0:T(8,128)(2,1)}), bf16[8192,128]{1,0:T(8,128)(2,1)}) %all-gather.9.cloned.1.call-update) | async-done | bytes 2097168 | tf_op jit(solution)/shard_map/all_gather | solution.py:115
  451.7 48.5 %while.50 = (s32[]{:T(128)}, f32[1,4,128]{2,1,0:T(4,128)S(1)}, f32[1,4,128]{2,1,0:T(4,128)S(1)}, f32[1,4,128,128]{3,2,1,0:T(8,128)S(1)}, s32[128]{0:T(128)S(1)},...) while((s32[]{:T(128)}, f32[1,4,128]{2,1,0:T(4,128)S(1)}, ...), condition=%wide.region_11.12_spmd.clone, body=%wide.region_8.11_spmd.clone.sunk | while | flops 136973952 | bytes 4363975 | solution.py:124
  453.1 1.4 fusion.91
  456.1 1.4 fusion.91
  459.2 1.4 fusion.91
  462.2 1.4 fusion.91
  465.2 1.4 fusion.91
  468.3 1.4 fusion.91
  471.3 1.4 fusion.91
  474.3 1.4 fusion.91
  477.4 1.4 fusion.91
  480.4 1.4 fusion.91
  483.4 1.4 fusion.91
  486.5 1.4 fusion.91
  492.5 1.4 fusion.91
  498.6 1.4 fusion.91
  503.1 105.1 %all-gather.13.cloned.1.call-done = bf16[256,128,128]{2,1,0:T(8,128)(2,1)} async-done(((bf16[4,128,128]{2,1,0:T(8,128)(2,1)}), bf16[256,128,128]{2,1,0:T(8,128)(2,1)}) %all-gather.13.cloned.1.call-update) | async-done | bytes 8388624 | tf_op jit(solution)/shard_map/all_gather | solution.py:18
  608.1 68.2 %while.49 = (s32[]{:T(128)}, f32[4,128,128]{2,1,0:T(8,128)S(1)}, s32[]{:T(128)}, bf16[64,4,128,128]{3,2,1,0:T(8,128)(2,1)}, s32[]{:T(128)}, /*index=5*/s32[]{:T(128)}, s32[]{:T(128)}, s32[]{:T(128)}) while((s32[]{:T(128)}, f32[4,128,128]{2,1,0:T(8,128)S(1)}, s32[]{:T(128)}, bf16[64,4,128,128]{3,2,1,0:T(8,128)(2,1)}, s32[]{:T(128)}, ...), condition=%wide.region_7.8_spmd.clone, body=%wide.region_6.7_spmd.clone.sunk | while | flops 262152 | bytes 655515 | solution.py:27
  (309 shorter events, 175.0 us)
Async XLA Ops:
  7.2 4.5 copy-start
  7.2 165.8 %all-gather.11.cloned.1.call-start = ((), (), s32[]{:S(2)}) async-start(), calls=%async_computation.2 | async-start | bytes 8519680 | tf_op jit(solution)/shard_map/all_gather | solution.py:18
  10.0 301.8 %all-gather.7.cloned.1.call-start = ((), (), s32[]{:S(2)}) async-start(), calls=%async_computation | async-start | bytes 2129920 | tf_op jit(solution)/shard_map/all_gather | solution.py:114
  10.8 440.9 %all-gather.9.cloned.1.call-start = ((), (), s32[]{:S(2)}) async-start(), calls=%async_computation.1 | async-start | bytes 2129920 | tf_op jit(solution)/shard_map/all_gather | solution.py:115
  11.5 596.6 %all-gather.13.cloned.1.call-start = ((), (), s32[]{:S(2)}) async-start(), calls=%async_computation.3 | async-start | bytes 8519680 | tf_op jit(solution)/shard_map/all_gather | solution.py:18
  173.0 78.5 %copy-start.2 = (bf16[128,512]{1,0:T(8,128)(2,1)S(1)}, bf16[128,512]{1,0:T(8,128)(2,1)}, u32[]{:S(2)}) copy-start(bf16[128,512]{1,0:T(8,128)(2,1)} %param.17) | copy-start | bytes 393220
  240.9 210.8 %copy-start.4 = (s32[128]{0:T(128)S(1)}, s32[128]{0:T(128)}, u32[]{:S(2)}) copy-start(s32[128]{0:T(128)} %param.21) | copy-start | bytes 1540
  451.7 49.4 %copy-start.1 = (bf16[128,512]{1,0:T(8,128)(2,1)S(1)}, bf16[128,512]{1,0:T(8,128)(2,1)}, u32[]{:S(2)}) copy-start(bf16[128,512]{1,0:T(8,128)(2,1)} %param.16) | copy-start | bytes 393220
  502.8 173.6 %copy-start.3 = (bf16[128,512]{1,0:T(8,128)(2,1)S(1)}, bf16[128,512]{1,0:T(8,128)(2,1)}, u32[]{:S(2)}) copy-start(bf16[128,512]{1,0:T(8,128)(2,1)} %param.15) | copy-start | bytes 393220
Sparse Core Ops, SparseCore 0:
  11.5 161.4 all-gather.10
  176.0 135.8 all-gather.6
  314.8 136.8 all-gather.8
  455.1 153.0 all-gather.12
where the time goes:
time: 688 us; the launch traced here: 685 us
  waiting for transfers between devices  449 us (65%)
  other arithmetic  140 us (20%)
  matrix products  47.7 us (7%)
  blocking collectives  23.2 us (3%)
  between operations  14 us (2%)
    all_gather x2, waiting for transfers between devices, carried_in(): everything = lax.all_gather(value.astype(jnp.bfloat16), axis)  263 us
    all_gather x1, waiting for transfers between devices, on_device(): value_rows = lax.all_gather(soft_value, 'ctx', axis=0, tiled=True)  140 us
    select_n x128, other arithmetic, hop(): return jnp.where(reached, new, before)  133 us
    all_gather x1, waiting for transfers between devices, on_device(): key_rows = lax.all_gather(soft_key, 'ctx', axis=0, tiled=True)  45 us
    dot_general x16, matrix products, attend(): jnp.einsum('kgtn,nkd->kgtd', probs.astype(jnp.bfloat16), value_heads, pre...  21.7 us
    dot_general x16, matrix products, attend(): jnp.einsum('tkgd,nkd->kgtn', soft_q, key_heads, preferred_element_type=jn...  19.5 us
  transfers between devices with their start and end apart: 4, of which 4 were waited for; matrix products, arithmetic and copies ran while one was open for 18% of the time, Pallas kernels for 0%

commit v1 on v0

--- a/solution.py
+++ b/solution.py
@@ -112,7 +112,15 @@
         jnp.zeros((kv_here, group, length, HD), jnp.float32),
     )
     key_rows = lax.all_gather(soft_key, "ctx", axis=0, tiled=True)
-    value_rows = lax.all_gather(soft_value, "ctx", axis=0, tiled=True)
+    value_rows = jnp.concatenate(
+        jax.lax.all_to_all(
+            jnp.stack(tuple((soft_value for _ in range(jax.lax.axis_size("ctx")))), axis=0),
+            split_axis=0,
+            axis_name="ctx",
+            concat_axis=0,
+        ),
+        0,
+    )
     count = key_rows.shape[0]
     block = math.gcd(count, 512)
 

time: 688 us -> 577 us (0.84)
  waiting for transfers between devices: 449 us -> 319 us
  starting transfers between devices: 0.16 us -> 19.2 us
    all_gather x1 -> x0, waiting for transfers between devices: 140 us -> none  [on_device(): value_rows = lax.all_gather(soft_value, 'ctx', axis=0, tiled=True)]
    all_to_all x0 -> x1, starting transfers between devices: none -> 19.1 us  [on_device(): jax.lax.all_to_all(jnp.stack(tuple((soft_value for _ in range(jax.lax.axi...]
    all_gather x2, waiting for transfers between devices: 263 us -> 274 us  [carried_in(): everything = lax.all_gather(value.astype(jnp.bfloat16), axis)]
  transfers between devices with their start and end apart: 4 -> 4, of which waited for: 4 -> 3; matrix products, arithmetic and copies ran while one was open for 18% -> 21% of each run, Pallas kernels for 0% -> 0%
where the time goes in v1:
time: 577 us; the launch traced here: 574 us
  waiting for transfers between devices  319 us (55%)
  other arithmetic  140 us (24%)
  matrix products  45.9 us (8%)
  blocking collectives  23.3 us (4%)
  starting transfers between devices  19.2 us (3%)
  between operations  14 us (2%)
  local copies, waits for them, and re-layouts  8.09 us (1%)
    all_gather x2, waiting for transfers between devices, carried_in(): everything = lax.all_gather(value.astype(jnp.bfloat16), axis)  274 us
    select_n x128, other arithmetic, hop(): return jnp.where(reached, new, before)  133 us
    all_gather x1, waiting for transfers between devices, on_device(): key_rows = lax.all_gather(soft_key, 'ctx', axis=0, tiled=True)  44.5 us
    dot_general x16, matrix products, attend(): jnp.einsum('kgtn,nkd->kgtd', probs.astype(jnp.bfloat16), value_heads, pre...  21.7 us
    dot_general x16, matrix products, attend(): jnp.einsum('tkgd,nkd->kgtn', soft_q, key_heads, preferred_element_type=jn...  19.6 us
    all_to_all x1, starting transfers between devices, on_device(): jax.lax.all_to_all(jnp.stack(tuple((soft_value for _ in range(jax.lax.axi...  19.1 us
    psum x1, blocking collectives, on_device(): inner = lax.psum(jnp.sum(grad * normed, axis=1), 'tp')  13.3 us
  transfers between devices with their start and end apart: 4, of which 3 were waited for; matrix products, arithmetic and copies ran while one was open for 21% of the time, Pallas kernels for 0%

profile of v1, /device:TPU:2, one launch (start us, length us, event | category | flops | bytes accessed | tf_op | source)
XLA Modules:
  0.0 573.8 jit_solution(14497119870010064305)
XLA Ops:
  8.3 1.7 convolution_convert_fusion.1
  10.0 2.6 stack.2
  12.7 19.1 %all-to-all-start = ((bf16[64,128,128]{2,1,0:T(8,128)(2,1)}), bf16[64,128,128]{2,1,0:T(8,128)(2,1)}, u32[]{:S(2)}, u32[]{:S(2)}) async-start(bf16[64,128,128]{2,1,0:T(8,128)(2,1)} %stack.2), calls=%async_computation | async-start | bytes 4194304 | tf_op jit(solution)/shard_map/all_to_all | solution.py:116
  33.4 168.2 %all-gather.8.cloned.1.call-done = bf16[256,128,128]{2,1,0:T(8,128)(2,1)} async-done(((bf16[4,128,128]{2,1,0:T(8,128)(2,1)}), bf16[256,128,128]{2,1,0:T(8,128)(2,1)}) %all-gather.8.cloned.1.call-update) | async-done | bytes 8388624 | tf_op jit(solution)/shard_map/all_gather | solution.py:18
  201.6 67.9 %while.48 = (s32[]{:T(128)}, f32[4,128,128]{2,1,0:T(8,128)S(1)}, s32[]{:T(128)}, bf16[64,4,128,128]{3,2,1,0:T(8,128)(2,1)}, s32[]{:T(128)}, /*index=5*/s32[]{:T(128)}) while((s32[]{:T(128)}, f32[4,128,128]{2,1,0:T(8,128)S(1)}, s32[]{:T(128)}, bf16[64,4,128,128]{3,2,1,0:T(8,128)(2,1)}, s32[]{:T(128)}, /*index=5*/s32[]{:T(128)}) %tuple.129), condition=%wide.region_1.2_spmd.clone, body=%wide.region_0.1_spmd.clone.sunk | while | flops 262148 | bytes 655453 | solution.py:27
  270.1 10.0 %psum.14 = f32[128]{0:T(128)S(1)} all-reduce(f32[128]{0:T(128)S(1)} %get-tuple-element.497), channel_id=1, replica_groups=mesh['ctx'=64,'tp'=8] {'tp'}, use_global_device_ids=true, to_apply=%region_3.4 | all-reduce | flops 128 | bytes 1024 | tf_op jit(solution)/shard_map/psum | solution.py:48
  280.3 13.3 %psum.15 = f32[128]{0:T(128)S(1)} all-reduce(f32[128]{0:T(128)S(1)} %fusion.30), channel_id=1, replica_groups=mesh['ctx'=64,'tp'=8] {'tp'}, use_global_device_ids=true, to_apply=%region_5.6 | all-reduce | flops 128 | bytes 1024 | tf_op jit(solution)/shard_map/psum | solution.py:53
  295.5 44.5 %all-gather.6.cloned.1.call-done = bf16[8192,128]{1,0:T(8,128)(2,1)} async-done(((bf16[128,128]{1,0:T(8,128)(2,1)}), bf16[8192,128]{1,0:T(8,128)(2,1)}) %all-gather.6.cloned.1.call-update) | async-done | bytes 2097168 | tf_op jit(solution)/shard_map/all_gather | solution.py:114
  339.9 48.5 %while.50 = (s32[]{:T(128)}, f32[1,4,128]{2,1,0:T(4,128)S(1)}, f32[1,4,128]{2,1,0:T(4,128)S(1)}, f32[1,4,128,128]{3,2,1,0:T(8,128)S(1)}, s32[128]{0:T(128)S(1)},...) while((s32[]{:T(128)}, f32[1,4,128]{2,1,0:T(4,128)S(1)}, ...), condition=%wide.region_11.12_spmd.clone, body=%wide.region_8.11_spmd.clone.sunk | while | flops 136973952 | bytes 4363975 | solution.py:132
  341.3 1.4 fusion.91
  344.4 1.4 fusion.91
  347.4 1.4 fusion.91
  350.4 1.4 fusion.91
  353.5 1.4 fusion.91
  356.5 1.4 fusion.91
  359.5 1.4 fusion.91
  362.6 1.4 fusion.91
  365.6 1.4 fusion.91
  368.6 1.4 fusion.91
  374.7 1.4 fusion.91
  377.7 1.4 fusion.91
  380.8 1.4 fusion.91
  391.3 105.5 %all-gather.10.cloned.1.call-done = bf16[256,128,128]{2,1,0:T(8,128)(2,1)} async-done(((bf16[4,128,128]{2,1,0:T(8,128)(2,1)}), bf16[256,128,128]{2,1,0:T(8,128)(2,1)}) %all-gather.10.cloned.1.call-update) | async-done | bytes 8388624 | tf_op jit(solution)/shard_map/all_gather | solution.py:18
  496.8 68.2 %while.49 = (s32[]{:T(128)}, f32[4,128,128]{2,1,0:T(8,128)S(1)}, s32[]{:T(128)}, bf16[64,4,128,128]{3,2,1,0:T(8,128)(2,1)}, s32[]{:T(128)}, /*index=5*/s32[]{:T(128)}, s32[]{:T(128)}, s32[]{:T(128)}) while((s32[]{:T(128)}, f32[4,128,128]{2,1,0:T(8,128)S(1)}, s32[]{:T(128)}, bf16[64,4,128,128]{3,2,1,0:T(8,128)(2,1)}, s32[]{:T(128)}, ...), condition=%wide.region_7.8_spmd.clone, body=%wide.region_6.7_spmd.clone.sunk | while | flops 262152 | bytes 655515 | solution.py:27
  (311 shorter events, 172.9 us)
Async XLA Ops:
  7.2 25.5 %copy-start = (bf16[128,512]{1,0:T(8,128)(2,1)S(1)}, bf16[128,512]{1,0:T(8,128)(2,1)}, u32[]{:S(2)}) copy-start(bf16[128,512]{1,0:T(8,128)(2,1)} %param.14) | copy-start | bytes 393220
  7.2 194.4 %all-gather.8.cloned.1.call-start = ((), (), s32[]{:S(2)}) async-start(), calls=%async_computation.2 | async-start | bytes 8519680 | tf_op jit(solution)/shard_map/all_gather | solution.py:18
  12.6 20.0 %copy-start.3 = (bf16[128,512]{1,0:T(8,128)(2,1)S(1)}, bf16[128,512]{1,0:T(8,128)(2,1)}, u32[]{:S(2)}) copy-start(bf16[128,512]{1,0:T(8,128)(2,1)} %param.15) | copy-start | bytes 393220
  12.6 20.3 %copy-start.1 = (bf16[128,512]{1,0:T(8,128)(2,1)S(1)}, bf16[128,512]{1,0:T(8,128)(2,1)}, u32[]{:S(2)}) copy-start(bf16[128,512]{1,0:T(8,128)(2,1)} %param.16) | copy-start | bytes 393220
  12.6 20.5 %copy-start.4 = (bf16[128,512]{1,0:T(8,128)(2,1)S(1)}, bf16[128,512]{1,0:T(8,128)(2,1)}, u32[]{:S(2)}) copy-start(bf16[128,512]{1,0:T(8,128)(2,1)} %param.18) | copy-start | bytes 393220
  12.7 327.3 %all-to-all-start = ((bf16[64,128,128]{2,1,0:T(8,128)(2,1)}), bf16[64,128,128]{2,1,0:T(8,128)(2,1)}, u32[]{:S(2)}, u32[]{:S(2)}) async-start(bf16[64,128,128]{2,1,0:T(8,128)(2,1)} %stack.2), calls=%async_computation | async-start | bytes 4194304 | tf_op jit(solution)/shard_map/all_to_all | solution.py:116
  31.8 308.1 %all-gather.6.cloned.1.call-start = ((), (), s32[]{:S(2)}) async-start(), calls=%async_computation.1 | async-start | bytes 2129920 | tf_op jit(solution)/shard_map/all_gather | solution.py:114
  32.5 464.2 %all-gather.10.cloned.1.call-start = ((), (), s32[]{:S(2)}) async-start(), calls=%async_computation.3 | async-start | bytes 8519680 | tf_op jit(solution)/shard_map/all_gather | solution.py:18
  201.6 78.5 %copy-start.2 = (bf16[128,512]{1,0:T(8,128)(2,1)S(1)}, bf16[128,512]{1,0:T(8,128)(2,1)}, u32[]{:S(2)}) copy-start(bf16[128,512]{1,0:T(8,128)(2,1)} %param.17) | copy-start | bytes 393220
  269.5 70.5 %copy-start.5 = (s32[128]{0:T(128)S(1)}, s32[128]{0:T(128)}, u32[]{:S(2)}) copy-start(s32[128]{0:T(128)} %param.21) | copy-start | bytes 1540
Sparse Core Ops, SparseCore 0:
  11.5 190.0 all-gather.7
  204.6 135.3 all-gather.5
  343.5 153.2 all-gather.9
